TPU v7x, 256 devices: a whole 4x4x8 slice. The times are simulated.
256 devices in a mesh: tm: 32 (over y, x, core), rows: 8 (over z).
Axes of the slice: x: 4, y: 4, z: 8, core: 2. Of those that a mesh axis runs over, the one named last changes fastest.
Arguments:
- features: bfloat16 [128, 64, 32, 512], P('tm', 'rows'), may hold values from -80 to 80
- gain_in: float32 [512], replicated, may hold values from 0.5 to 2
- shift_in: float32 [512], replicated, may hold values from -3 to 3
- conv_in: bfloat16 [3, 3, 3, 512, 256], replicated, may hold values from -0.0546875 to 0.0546875
- gain_mid: float32 [256], replicated, may hold values from 0.5 to 2
- shift_mid: float32 [256], replicated, may hold values from -3 to 3
- conv_out: bfloat16 [3, 3, 3, 256, 256], replicated, may hold values from -0.078125 to 0.078125
- shortcut: bfloat16 [512, 256], replicated, may hold values from -0.25 to 0.25
Outputs:
- decoded: bfloat16 [128, 64, 32, 256], P('tm', 'rows')
All inputs are finite; a program needn't handle non-finite values.
Results may differ from a plain program's by a relative error of at most 0.012.
Values may be sent and summed in bfloat16 or wider, within the bound.
A program may use at most 128 MiB of HBM per device.

v0:
```python
import jax
import jax.numpy as jnp
from jax import lax
from jax.sharding import PartitionSpec as P

GROUPS = 32


epsilon = 1e-06


def shifted(block, axis, distance):
    devices = range(lax.axis_size(axis))
    route = [(i - distance, i) for i in devices if i - distance in devices]
    return lax.ppermute(block, axis, route)


def extended_2(cells, sides, width):
    for axis, dim in sides:
        count = lax.axis_size(axis)
        ends = count - 1
        head = lax.slice_in_dim(cells, 0, width, axis=dim)
        tail = lax.slice_in_dim(cells, cells.shape[dim] - width, cells.shape[dim], axis=dim)
        cells = jnp.concatenate(
            [
                lax.ppermute(tail, axis, [(i, (i + 1) % count) for i in range(ends)]),
                cells,
                lax.ppermute(head, axis, [((i + 1) % count, i) for i in range(ends)]),
            ],
            axis=dim,
        )
    return cells


def conv_block(extended, kernel):
    out_frames = extended.shape[0] - 2
    out_rows = extended.shape[1] - 2
    out_cols = extended.shape[2] - 2
    channels = extended.shape[3]
    width_out = kernel.shape[4]
    summed = jnp.zeros((out_frames * out_rows * out_cols, width_out), jnp.float32)
    for offset_time in range(3):
        for offset_row in range(3):
            stacked = jnp.concatenate(
                [
                    extended[
                        offset_time : offset_time + out_frames,
                        offset_row : offset_row + out_rows,
                        offset_col : offset_col + out_cols,
                        :,
                    ]
                    for offset_col in range(3)
                ],
                axis=-1,
            )
            matrix = kernel[offset_time, offset_row].reshape(3 * channels, width_out)
            summed = summed + jnp.dot(
                stacked.reshape(-1, 3 * channels), matrix, preferred_element_type=jnp.float32
            )
    return summed.reshape(out_frames, out_rows, out_cols, width_out)


def grouped(values):
    return values.astype(jnp.float32).reshape(
        values.shape[:-1] + (GROUPS, values.shape[-1] // GROUPS)
    )


def statistics(values, first_norm):
    shaped = grouped(values)
    cell_count = (
        values.shape[0]
        * values.shape[1]
        * values.shape[2]
        * lax.axis_size("tm")
        * lax.axis_size("rows")
        * shaped.shape[-1]
    )
    partial_sum = jnp.sum(shaped, axis=(0, 1, 2, 4))
    if first_norm:
        group_mean = lax.psum(partial_sum, ("tm", "rows")) / cell_count
    else:
        group_mean = lax.psum(partial_sum, ("tm", "rows")) / cell_count
    partial_spread = jnp.sum(jnp.square(shaped - group_mean[:, None]), axis=(0, 1, 2, 4))
    if first_norm:
        group_var = lax.psum(partial_spread, ("tm", "rows")) / cell_count
    else:
        group_var = lax.psum(partial_spread, ("tm", "rows")) / cell_count
    return (group_mean, group_var)


def activate(values, group_mean, group_var, gain, shift):
    shaped = grouped(values)
    normed = (shaped - group_mean[:, None]) * lax.rsqrt(group_var[:, None] + epsilon)
    normed = normed.reshape(values.shape) * gain + shift
    return jax.nn.silu(normed).astype(jnp.bfloat16)


def pad_columns(values):
    return jnp.pad(values, ((0, 0), (0, 0), (1, 1), (0, 0)))


def opening(received, values):
    starting = lax.axis_index("tm") == 0
    copies = jnp.broadcast_to(values[:1], received.shape)
    return jnp.where(starting, copies, received)


def per_device(features, gain_in, shift_in, conv_in, gain_mid, shift_mid, conv_out, shortcut):
    mean_in, var_in = statistics(features, True)
    first = activate(features, mean_in, var_in, gain_in, shift_in)
    earlier = shifted(first[-2:], "tm", 1)
    earlier = opening(earlier, first)
    extended = jnp.concatenate([earlier, first], axis=0)
    rimmed = extended_2(extended, (("rows", 1),), 1)
    hidden = conv_block(pad_columns(rimmed), conv_in).astype(jnp.bfloat16)
    mean_mid, var_mid = statistics(hidden, False)
    second = activate(hidden, mean_mid, var_mid, gain_mid, shift_mid)
    later_tail = shifted(second[-2:], "tm", 1)
    later_tail = opening(later_tail, second)
    second_ext = jnp.concatenate([later_tail, second], axis=0)
    rimmed_mid = extended_2(second_ext, (("rows", 1),), 1)
    branch = conv_block(pad_columns(rimmed_mid), conv_out)
    skipped = jnp.dot(
        features.reshape(-1, features.shape[-1]), shortcut, preferred_element_type=jnp.float32
    ).reshape(branch.shape)
    return (branch + skipped).astype(jnp.bfloat16)


def solution(mesh):
    return jax.shard_map(
        per_device,
        mesh=mesh,
        in_specs=(P("tm", "rows", None, None), P(), P(), P(), P(), P(), P(), P()),
        out_specs=P("tm", "rows", None, None),
        check_vma=False,
    )
```

profile of v0, /device:TPU:1, one launch (start us, length us, event | category | flops | bytes accessed | tf_op | source)
XLA Modules:
  0.0 388.2 jit_solution(10099166680789277011)
XLA Ops:
  0.0 1.5 convert_reduce_fusion
  1.7 81.4 %psum.28 = f32[32]{0:T(128)S(1)} all-reduce(f32[32]{0:T(128)S(1)} %reduce_sum.51), channel_id=1, replica_groups=mesh['tm'=32,'rows'=8] {'tm','rows'}, use_global_device_ids=true, to_apply=%region_2.0 | all-reduce | flops 32 | bytes 256 | tf_op jit(solution)/shard_map/psum | solution.py:81
  83.3 1.6 fusion.9
  85.0 72.4 %psum.29 = f32[32]{0:T(128)S(1)} all-reduce(f32[32]{0:T(128)S(1)} %reduce_sum.54), channel_id=1, replica_groups=mesh['tm'=32,'rows'=8] {'tm','rows'}, use_global_device_ids=true, to_apply=%region_5.6 | all-reduce | flops 32 | bytes 256 | tf_op jit(solution)/shard_map/psum | solution.py:86
  157.6 2.0 fusion.17
  159.6 2.8 collective-permute-start
  162.5 6.1 %collective-permute-done = bf16[2,8,32,512]{3,2,1,0:T(8,128)(2,1)S(1)} collective-permute-done((bf16[2,8,32,512]{3,2,1,0:T(8,128)(2,1)S(1)}, bf16[2,8,32,512]{3,2,1,0:T(8,128)(2,1)S(1)}, u32[]{:S(2)}, u32[]{:S(2)}) %collective-permute-start) | collective-permute-done | bytes 524320 | tf_op jit(solution)/shard_map/ppermute | solution.py:15
  168.7 1.3 collective-permute-start.2
  170.0 4.5 %collective-permute-start.1 = (bf16[6,1,32,512]{3,2,1,0:T(8,128)(2,1)S(1)}, bf16[6,1,32,512]{3,2,1,0:T(8,128)(2,1)S(1)}, u32[]{:S(2)}, u32[]{:S(2)}) collective-permute-start(bf16[6,1,32,512]{3,2,1,0:T(8,128)(2,1)S(1)} %get-tuple-element.49), channel_id=1, source_target_pairs={{0,1},{1,2},{2,3},{3,4},{4,5},{5,6},{6,7},{8,9},{9,10},{10,11},{11... | collective-permute-start | bytes 589832 | tf_op jit(solution)/shard_map/ppermute | solution.py:26
  174.5 5.9 %fusion.31 = (bf16[1,1,3,512,256]{4,3,2,1,0:T(8,128)(2,1)}, bf16[1,1,3,512,256]{4,3,2,1,0:T(8,128)(2,1)}, bf16[1,1,3,512,256]{4,3,2,1,0:T(8,128)(2,1)}, bf16[1,1...) fusion(bf16[3,3,3,512,256]{4,3,2,1,0:T(8,128)(2,1)} %param.11), kind=kLoop, calls=%fused_computation.96 | loop fusion | bytes 14155776 | tf_op jit(solution)/shard_map/slice | solution.py:56
  180.4 1.1 fusion.28
  181.5 1.4 select_maximum_fusion
  182.9 6.2 %fusion.33 = (bf16[4,8,32,512]{3,2,1,0:T(8,128)(2,1)S(1)}, bf16[4,8,32,512]{3,2,1,0:T(8,128)(2,1)S(1)}, bf16[4,8,32,512]{3,2,1,0:T(8,128)(2,1)S(1)}, bf16[4,8,32...) fusion(bf16[6,10,34,512]{3,2,1,0:T(8,128)(2,1)S(1)} %select_max, ...), kind=kLoop, calls=%fused_computation.98 | loop fusion | bytes 37748736 | tf_op jit(solution)/shard_map/slice | solution.py:46
  189.2 0.5 maximum_maximum_fusion
  189.7 0.8 fusion.34
  190.5 0.4 copy-done.9
  190.9 0.3 copy-done.10
  191.5 0.8 copy-done.20
  192.3 1.0 fusion.41
  193.5 0.3 copy-done.8
  193.9 0.3 copy-done.11
  194.2 0.3 pad_maximum_fusion.2
  194.5 0.8 copy-done.19
  195.3 1.0 fusion.40
  196.5 0.3 copy-done.6
  196.9 0.3 pad_maximum_fusion.1
  197.2 0.8 copy-done.18
  198.0 1.0 convolution_add_fusion.14
  199.2 0.3 copy-done.4
  199.5 0.3 pad_maximum_fusion.3
  199.8 0.8 copy-done.17
  200.7 1.0 convolution_add_fusion.13
  202.2 0.8 copy-done.16
  203.0 1.0 convolution_add_fusion.12
  204.3 0.5 pad_maximum_fusion.7
  204.9 0.6 copy-done.12
  205.4 1.0 fusion.21
  206.6 1.0 convolution_add_fusion.10
  207.7 1.0 convolution_add_fusion.9
  209.0 0.8 copy-done.13
  209.9 1.0 fusion.39
  211.1 77.8 %psum.30 = f32[32]{0:T(128)S(1)} all-reduce(f32[32]{0:T(128)S(1)} %reduce_sum.72), channel_id=1, replica_groups=mesh['tm'=32,'rows'=8] {'tm','rows'}, use_global_device_ids=true, to_apply=%region_8.9 | all-reduce | flops 32 | bytes 256 | tf_op jit(solution)/shard_map/psum | solution.py:83
  289.5 72.2 %psum.31 = f32[32]{0:T(128)S(1)} all-reduce(f32[32]{0:T(128)S(1)} %reduce_sum.75), channel_id=1, replica_groups=mesh['tm'=32,'rows'=8] {'tm','rows'}, use_global_device_ids=true, to_apply=%region_11.12 | all-reduce | flops 32 | bytes 256 | tf_op jit(solution)/shard_map/psum | solution.py:88
  361.9 0.3 multiply_convert_fusion
  362.3 2.8 collective-permute-start.3
  365.1 2.3 fusion.32
  367.5 0.9 collective-permute-done.3
  368.5 1.3 collective-permute-start.5
  369.8 4.3 %collective-permute-start.4 = (bf16[6,1,32,256]{3,2,1,0:T(8,128)(2,1)S(1)}, bf16[6,1,32,256]{3,2,1,0:T(8,128)(2,1)S(1)}, u32[]{:S(2)}, u32[]{:S(2)}) collective-permute-start(bf16[6,1,32,256]{3,2,1,0:T(8,128)(2,1)S(1)} %get-tuple-element.79), channel_id=1, source_target_pairs={{0,1},{1,2},{2,3},{3,4},{4,5},{5,6},{6,7},{8,9},{9,10},{10,11},{11... | collective-permute-start | bytes 294920 | tf_op jit(solution)/shard_map/ppermute | solution.py:26
  374.2 1.6 collective-permute-done.4
  375.8 0.7 select_maximum_fusion.2
  376.5 3.0 fusion.36
  380.1 0.6 fusion.43
  380.8 0.6 fusion.42
  381.5 0.6 convolution_add_fusion.6
  382.2 0.6 convolution_add_fusion.5
  382.9 0.6 convolution_add_fusion.4
  383.6 0.3 pad_maximum_fusion.17
  383.9 0.6 fusion.20
  384.5 0.6 convolution_add_fusion.2
  385.1 0.6 convolution_add_fusion.1
  385.9 0.6 convolution_add_fusion
  386.5 0.5 copy-done.1
  387.0 1.2 fusion.22
  (79 shorter events, 5.5 us)
Async XLA Ops:
  0.0 386.5 %copy-start = (bf16[512,256]{1,0:T(8,128)(2,1)S(1)}, bf16[512,256]{1,0:T(8,128)(2,1)}, u32[]{:S(2)}) copy-start(bf16[512,256]{1,0:T(8,128)(2,1)} %param.15) | copy-start | bytes 786436
  159.6 9.0 %collective-permute-start = (bf16[2,8,32,512]{3,2,1,0:T(8,128)(2,1)S(1)}, bf16[2,8,32,512]{3,2,1,0:T(8,128)(2,1)S(1)}, u32[]{:S(2)}, u32[]{:S(2)}) collective-permute-start(bf16[2,8,32,512]{3,2,1,0:T(8,128)(2,1)S(1)} %slice.351), channel_id=1, source_target_pairs={{0,8},{8,16},{16,24},{24,32},{32,40},{40,48},{48,56},{56,64},{64,7... | collective-permute-start | bytes 1572872 | tf_op jit(solution)/shard_map/ppermute | solution.py:15
  168.7 12.8 %collective-permute-start.2 = (bf16[6,1,32,512]{3,2,1,0:T(8,128)(2,1)S(1)}, bf16[6,1,32,512]{3,2,1,0:T(8,128)(2,1)S(1)}, u32[]{:S(2)}, u32[]{:S(2)}) collective-permute-start(bf16[6,1,32,512]{3,2,1,0:T(8,128)(2,1)S(1)} %get-tuple-element.50), channel_id=1, source_target_pairs={{1,0},{2,1},{3,2},{4,3},{5,4},{6,5},{7,6},{9,8},{10,9},{11,10},{12... | collective-permute-start | bytes 589832 | tf_op jit(solution)/shard_map/ppermute | solution.py:28
  170.0 11.5 %collective-permute-start.1 = (bf16[6,1,32,512]{3,2,1,0:T(8,128)(2,1)S(1)}, bf16[6,1,32,512]{3,2,1,0:T(8,128)(2,1)S(1)}, u32[]{:S(2)}, u32[]{:S(2)}) collective-permute-start(bf16[6,1,32,512]{3,2,1,0:T(8,128)(2,1)S(1)} %get-tuple-element.49), channel_id=1, source_target_pairs={{0,1},{1,2},{2,3},{3,4},{4,5},{5,6},{6,7},{8,9},{9,10},{10,11},{11... | collective-permute-start | bytes 589832 | tf_op jit(solution)/shard_map/ppermute | solution.py:26
  189.6 1.2 copy-start.9
  189.7 1.5 copy-start.10
  191.2 1.1 copy-start.20
  192.3 1.2 copy-start.7
  192.3 1.5 copy-start.8
  192.3 1.9 copy-start.11
  194.2 1.1 copy-start.19
  195.3 1.2 copy-start.5
  195.3 1.5 copy-start.6
  196.8 1.1 copy-start.18
  198.0 1.2 copy-start.3
  198.0 1.5 copy-start.4
  199.5 1.1 copy-start.17
  200.7 1.2 copy-start.2
  201.9 1.1 copy-start.16
  204.3 1.1 copy-start.12
  205.4 1.1 copy-start.15
  206.6 1.1 copy-start.14
  208.7 1.1 copy-start.13
  209.9 152.0 %copy-start.21 = (f32[256]{0:T(256)S(1)}, f32[256]{0:T(256)}, u32[]{:S(2)}) copy-start(f32[256]{0:T(256)} %param.13) | copy-start | bytes 3076
  209.9 152.0 %copy-start.22 = (f32[256]{0:T(256)S(1)}, f32[256]{0:T(256)}, u32[]{:S(2)}) copy-start(f32[256]{0:T(256)} %param.12) | copy-start | bytes 3076
  362.3 6.1 %collective-permute-start.3 = (bf16[2,8,32,256]{3,2,1,0:T(8,128)(2,1)S(1)}, bf16[2,8,32,256]{3,2,1,0:T(8,128)(2,1)S(1)}, u32[]{:S(2)}, u32[]{:S(2)}) collective-permute-start(bf16[2,8,32,256]{3,2,1,0:T(8,128)(2,1)S(1)} %slice.379), channel_id=1, source_target_pairs={{0,8},{8,16},{16,24},{24,32},{32,40},{40,48},{48,56},{56,64},{64,7... | collective-permute-start | bytes 786440 | tf_op jit(solution)/shard_map/ppermute | solution.py:15
  368.5 5.7 %collective-permute-start.5 = (bf16[6,1,32,256]{3,2,1,0:T(8,128)(2,1)S(1)}, bf16[6,1,32,256]{3,2,1,0:T(8,128)(2,1)S(1)}, u32[]{:S(2)}, u32[]{:S(2)}) collective-permute-start(bf16[6,1,32,256]{3,2,1,0:T(8,128)(2,1)S(1)} %get-tuple-element.80), channel_id=1, source_target_pairs={{1,0},{2,1},{3,2},{4,3},{5,4},{6,5},{7,6},{9,8},{10,9},{11,10},{12... | collective-permute-start | bytes 294920 | tf_op jit(solution)/shard_map/ppermute | solution.py:28
  369.8 6.0 %collective-permute-start.4 = (bf16[6,1,32,256]{3,2,1,0:T(8,128)(2,1)S(1)}, bf16[6,1,32,256]{3,2,1,0:T(8,128)(2,1)S(1)}, u32[]{:S(2)}, u32[]{:S(2)}) collective-permute-start(bf16[6,1,32,256]{3,2,1,0:T(8,128)(2,1)S(1)} %get-tuple-element.79), channel_id=1, source_target_pairs={{0,1},{1,2},{2,3},{3,4},{4,5},{5,6},{6,7},{8,9},{9,10},{10,11},{11... | collective-permute-start | bytes 294920 | tf_op jit(solution)/shard_map/ppermute | solution.py:26
  385.7 1.2 copy-start.1
where the time goes:
time: 392 us; the launch traced here: 388 us
  blocking collectives  304 us (78%)
  local copies, waits for them, and re-layouts  28.9 us (7%)
  starting transfers between devices  17.1 us (4%)
  matrix products  15.4 us (4%)
  other arithmetic  13.7 us (3%)
  waiting for transfers between devices  8.67 us (2%)
    psum x2, blocking collectives, statistics(): group_mean = lax.psum(partial_sum, ('tm', 'rows')) / cell_count  159 us
    psum x2, blocking collectives, statistics(): group_var = lax.psum(partial_spread, ('tm', 'rows')) / cell_count  145 us
    dot_general x18, matrix products, conv_block(): jnp.dot(stacked.reshape(-1, 3 * channels), matrix, preferred_element_type...  14.2 us
    slice x5, local copies, waits for them, and re-layouts, conv_block(): extended[offset_time:offset_time + out_frames, offset_row:offset_row + ou...  10.3 us
    unnamed x46, local copies, waits for them, and re-layouts  9.29 us
    ppermute x2, starting transfers between devices, extended_2(): lax.ppermute(tail, axis, [(i, (i + 1) % count) for i in range(ends)])  8.82 us
    slice x2, local copies, waits for them, and re-layouts, conv_block(): matrix = kernel[offset_time, offset_row].reshape(3 * channels, width_out)  8.24 us
  transfers between devices with their start and end apart: 6, of which 3 were waited for; matrix products, arithmetic and copies ran while one was open for 2% of the time, Pallas kernels for 0%

commit v1 on v0

v1 whole, which is shorter than its diff:
```python
import itertools

import jax
import jax.numpy as jnp
from jax import lax
from jax.experimental import pallas as pl
from jax.experimental.pallas import tpu as pltpu
from jax.sharding import PartitionSpec as P

GROUPS = 32
FRAMES = 4
ROWS = 8
COLS = 32
CELLS = FRAMES * ROWS * COLS
EPSILON = 1e-06
F32 = jnp.float32
BF16 = jnp.bfloat16
MESH = pl.DeviceIdType.MESH
SIZES = {"y": 4, "x": 4, "core": 2, "z": 8}
STAGES = (("z", "core"), ("y", "x"))
HOPS = {2: (0, 1), 4: (0, 1, 2, 1), 8: (0, 1, 2, 3, 4, 3, 2, 1)}


def offsets(axes):
    every = itertools.product(*[range(SIZES[a]) for a in axes])
    moved = [o for o in every if any(o)]
    return sorted(moved, key=lambda o: -sum(HOPS[SIZES[a]][i] for a, i in zip(axes, o)))


def group_sum(values, width):
    lane = lax.broadcasted_iota(jnp.int32, values.shape, 1)
    step = 1
    while step < width:
        up = pltpu.roll(values, 128 - step, 1)
        down = pltpu.roll(values, step, 1)
        values = values + jnp.where((lane // step) % 2 == 0, up, down)
        step *= 2
    return values


def to_rows(values):
    return jnp.concatenate([values[:, i : i + 128] for i in range(0, values.shape[1], 128)], axis=0)


def to_lanes(values):
    return jnp.concatenate([values[i : i + 1, :] for i in range(values.shape[0])], axis=1)


def local_statistics(ext):
    channels = ext.shape[-1]
    width = channels // GROUPS
    rows = channels // 128

    def slab(i):
        return ext[2 + i // ROWS, 1 + i % ROWS].astype(F32)

    def add_up(i, total):
        return total + slab(i).reshape(COLS // 8, 8, channels).sum(0)

    zero = jnp.zeros((8, channels), F32)
    total = lax.fori_loop(0, FRAMES * ROWS, add_up, zero, unroll=4).sum(0, keepdims=True)
    mean = group_sum(to_rows(total), width) * (1.0 / (CELLS * width))
    wide_mean = to_lanes(mean)

    def add_square(i, total):
        return total + jnp.square(slab(i) - wide_mean).reshape(COLS // 8, 8, channels).sum(0)

    spread = lax.fori_loop(0, FRAMES * ROWS, add_square, zero, unroll=4).sum(0, keepdims=True)
    spread = group_sum(to_rows(spread), width)
    lane = lax.broadcasted_iota(jnp.int32, (1, 128), 1)
    packed = jnp.zeros((1, 128), F32)
    for r in range(rows):
        both = jnp.where(lane % 4 < 2, mean[r : r + 1], spread[r : r + 1])
        packed = packed + jnp.where((lane % width) // 4 == r, both, 0.0)
    return packed


def combined(own, others, count):
    members = others.shape[0] + 1
    lane = lax.broadcasted_iota(jnp.int32, (1, 128), 1)
    total = own + jnp.sum(others, axis=0)
    mean = total * (1.0 / members)
    deviation = jnp.square(own - mean) + jnp.sum(jnp.square(others - mean[None]), axis=0)
    moved = pltpu.roll(deviation, 2, 1)
    return jnp.where(lane % 4 < 2, mean, total + moved * float(count))


def unpacked(packed, channels):
    width = channels // GROUPS
    rows = channels // 128
    shape = (2 * rows, 128)
    lane = lax.broadcasted_iota(jnp.int32, shape, 1)
    row = lax.broadcasted_iota(jnp.int32, shape, 0)
    wanted = jnp.where(row < rows, 4 * row, 4 * (row - rows) + 2)
    picked = jnp.where(lane % width == wanted, jnp.broadcast_to(packed, shape), 0.0)
    spread = group_sum(picked, width)
    return spread[:rows], spread[rows:]


def activate_slab(raw, out, frame, row, mean, scale, shift):
    v = (raw[frame, row].astype(F32) - mean) * scale + shift
    out[frame, row] = (v + v * jnp.tanh(v)).astype(BF16)


def convolve(act, weights, acc, first_frame, frames):
    channels = act.shape[-1]
    cells = frames * ROWS * COLS

    def one_column_tap(e, carry):
        taps = [
            act[first_frame + a : first_frame + a + frames, b : b + ROWS].reshape(cells, channels)
            for a in range(3)
            for b in range(3)
        ]
        matrix = weights[:, :, e].reshape(9 * channels, weights.shape[-1])
        acc[e, 0:cells] = jnp.dot(
            jnp.concatenate(taps, axis=-1), matrix, preferred_element_type=F32
        )
        return carry

    lax.fori_loop(0, 3, one_column_tap, 0)
    left, middle, right = acc[0, 0:cells], acc[1, 0:cells], acc[2, 0:cells]
    col = lax.broadcasted_iota(jnp.int32, left.shape, 0) % COLS
    from_left = jnp.where(col == 0, 0.0, pltpu.roll(left, 1, 0))
    from_right = jnp.where(col == COLS - 1, 0.0, pltpu.roll(right, cells - 1, 0))
    return middle + from_left + from_right


def kernel(
    x_hbm, gain_in_hbm, shift_in_hbm, w1_hbm, gain_mid_hbm, shift_mid_hbm, w2_hbm, short_hbm,
    out_ref,
    xr, xa, hr, ha, w1, w2, short, acc, skip, gain_in, shift_in, gain_mid, shift_mid,
    stat_out, stat_in_a, stat_in_b,
    load_sem, stat_send, stat_recv, x_send, x_recv, h_send, h_recv,
):
    tm = lax.axis_index("tm")
    z = lax.axis_index("rows")
    last_tm = lax.axis_size("tm") - 1
    last_z = lax.axis_size("rows") - 1
    here = {"y": tm // 8, "x": (tm // 2) % 4, "core": tm % 2, "z": z}

    def partner(axes, offset):
        there = dict(here)
        for a, o in zip(axes, offset):
            there[a] = lax.rem(here[a] + o, SIZES[a])
        return ((there["y"] * 4 + there["x"]) * 2 + there["core"], there["z"])

    barrier = pltpu.get_barrier_semaphore()
    stage_partners = [[partner(axes, o) for o in offsets(axes)] for axes in STAGES]

    loads = [
        pltpu.make_async_copy(src, dst, load_sem.at[i])
        for i, (src, dst) in enumerate(
            [
                (x_hbm, xr.at[2:6, 1:9]),
                (gain_in_hbm, gain_in),
                (shift_in_hbm, shift_in),
                (short_hbm, short),
                (w1_hbm, w1),
                (gain_mid_hbm, gain_mid),
                (shift_mid_hbm, shift_mid),
                (w2_hbm, w2),
            ]
        )
    ]
    for load in loads:
        load.start()

    for target in itertools.chain(*stage_partners):
        pl.semaphore_signal(barrier, inc=1, device_id=target, device_id_type=MESH)

    def greet(ok, target):
        @pl.when(ok)
        def _():
            pl.semaphore_signal(barrier, inc=1, device_id=target, device_id_type=MESH)

    greet(tm > 0, (tm - 1, z))
    greet((tm > 0) & (z > 0), (tm - 1, z - 1))
    greet((tm > 0) & (z < last_z), (tm - 1, z + 1))

    has_next = tm < last_tm
    has_prev = tm > 0
    has_above = z > 0
    has_below = z < last_z

    def halo_copies(src, ext, send, recv, parts):
        frames = {"all": (0, 4), "late": (2, 4), "early": (0, 2)}
        made = []
        for part in parts:
            kind, span, slot = part
            lo, hi = frames[span]
            if kind == "next":
                made.append(
                    (has_next, has_prev, src(2, 4, 0, 8), ext.at[0:2, 1:9], (tm + 1, z), slot)
                )
            elif kind == "down":
                made.append(
                    (has_below, has_above, src(lo, hi, 7, 8), ext.at[2 + lo : 2 + hi, 0:1],
                     (tm, z + 1), slot)
                )
            elif kind == "up":
                made.append(
                    (has_above, has_below, src(lo, hi, 0, 1), ext.at[2 + lo : 2 + hi, 9:10],
                     (tm, z - 1), slot)
                )
            elif kind == "next_down":
                made.append(
                    (has_next & has_below, has_prev & has_above, src(2, 4, 7, 8),
                     ext.at[0:2, 0:1], (tm + 1, z + 1), slot)
                )
            else:
                made.append(
                    (has_next & has_above, has_prev & has_below, src(2, 4, 0, 1),
                     ext.at[0:2, 9:10], (tm + 1, z - 1), slot)
                )
        copies = []
        for sends, gets, source, target, device, slot in made:
            copy = pltpu.make_async_remote_copy(
                src_ref=source, dst_ref=target, send_sem=send.at[slot], recv_sem=recv.at[slot],
                device_id=device, device_id_type=MESH,
            )
            copies.append((sends, gets, copy))
        return copies

    def start(copies):
        for sends, _, copy in copies:
            pl.when(sends)(copy.start)

    def wait_sent(copies):
        for sends, _, copy in copies:
            pl.when(sends)(copy.wait_send)

    def wait_received(copies):
        for _, gets, copy in copies:
            pl.when(gets)(copy.wait_recv)

    def stat_copies(which, stage):
        buffer = (stat_in_a, stat_in_b)[stage]
        return [
            pltpu.make_async_remote_copy(
                src_ref=stat_out.at[which, stage], dst_ref=buffer.at[which, i],
                send_sem=stat_send.at[which, stage], recv_sem=stat_recv.at[which, stage],
                device_id=target, device_id_type=MESH,
            )
            for i, target in enumerate(stage_partners[stage])
        ]

    def exchange(which, packed, count, meanwhile):
        for stage in range(2):
            buffer = (stat_in_a, stat_in_b)[stage]
            stat_out[which, stage] = packed
            for copy in stat_copies(which, stage):
                copy.start()
            meanwhile(stage)
            pltpu.make_async_copy(
                buffer.at[which], buffer.at[which], stat_recv.at[which, stage]
            ).wait()
            packed = combined(packed, buffer[which], count)
            count = count * (buffer.shape[1] + 1)
        return packed, count

    def coefficients(packed, count, channels, gain, shift):
        mean, spread = unpacked(packed, channels)
        inverse = lax.rsqrt(spread * (1.0 / count) + EPSILON)
        return to_lanes(mean), 0.5 * gain[...] * to_lanes(inverse), 0.5 * shift[...]

    def activate_own(raw, out, mean, scale, shift):
        def body(i, carry):
            activate_slab(raw, out, 2 + i // ROWS, 1 + i % ROWS, mean, scale, shift)
            return carry

        lax.fori_loop(0, FRAMES * ROWS, body, 0, unroll=2)

    def activate_edges(raw, out, lo, hi, mean, scale, shift):
        for row, ok in ((0, has_above), (9, has_below)):

            @pl.when(ok)
            def _():
                def body(f, carry):
                    activate_slab(raw, out, f, row, mean, scale, shift)
                    return carry

                lax.fori_loop(lo, hi, body, 0)

            @pl.when(jnp.logical_not(ok))
            def _():
                out[lo:hi, row] = jnp.zeros((hi - lo, COLS, out.shape[-1]), BF16)

    def activate_past(raw, out, mean, scale, shift):
        @pl.when(has_prev)
        def _():
            def body(i, carry):
                activate_slab(raw, out, i // ROWS, 1 + i % ROWS, mean, scale, shift)
                return carry

            lax.fori_loop(0, 2 * ROWS, body, 0, unroll=2)
            activate_edges(raw, out, 0, 2, mean, scale, shift)

        @pl.when(jnp.logical_not(has_prev))
        def _():
            def body(r, carry):
                out[0, r] = out[2, r]
                out[1, r] = out[2, r]
                return carry

            lax.fori_loop(0, ROWS + 2, body, 0)

    x_copies = halo_copies(
        lambda f0, f1, r0, r1: x_hbm.at[f0:f1, r0:r1], xr, x_send, x_recv,
        [("down", "all", 0), ("up", "all", 1), ("next", "all", 2),
         ("next_down", "all", 3), ("next_up", "all", 4)],
    )

    def own_hidden(f0, f1, r0, r1):
        return hr.at[2 + f0 : 2 + f1, 1 + r0 : 1 + r1]

    h_late = halo_copies(
        own_hidden, hr, h_send, h_recv,
        [("next", "all", 0), ("next_down", "all", 1), ("next_up", "all", 2),
         ("down", "late", 3), ("up", "late", 4)],
    )
    h_early = halo_copies(
        own_hidden, hr, h_send, h_recv, [("down", "early", 5), ("up", "early", 6)]
    )

    loads[0].wait()
    packed = local_statistics(xr)
    pl.semaphore_wait(
        barrier,
        sum(len(p) for p in stage_partners)
        + has_next.astype(jnp.int32)
        + (has_next & has_above).astype(jnp.int32)
        + (has_next & has_below).astype(jnp.int32),
    )

    def during_first(stage):
        if stage == 0:
            loads[3].wait()
            skip[...] = jnp.dot(
                xr[2:6, 1:9].reshape(CELLS, xr.shape[-1]), short[...], preferred_element_type=F32
            )
        if stage == 1:
            start(x_copies)

    packed, count = exchange(0, packed, CELLS * (xr.shape[-1] // GROUPS), during_first)
    loads[1].wait()
    loads[2].wait()
    mean, scale, shift = coefficients(packed, count, xr.shape[-1], gain_in, shift_in)
    activate_own(xr, xa, mean, scale, shift)
    wait_received(x_copies[:2])
    activate_edges(xr, xa, 2, 6, mean, scale, shift)
    loads[4].wait()
    hidden = convolve(xa, w1, acc, 2, 2)
    hr[4:6, 1:9] = hidden.reshape(2, ROWS, COLS, hidden.shape[-1]).astype(BF16)
    start(h_late)
    wait_received(x_copies[2:])
    activate_past(xr, xa, mean, scale, shift)
    hidden = convolve(xa, w1, acc, 0, 2)
    hr[2:4, 1:9] = hidden.reshape(2, ROWS, COLS, hidden.shape[-1]).astype(BF16)

    packed = local_statistics(hr)

    def during_second(stage):
        if stage == 0:
            start(h_early)

    packed, count = exchange(1, packed, CELLS * (hr.shape[-1] // GROUPS), during_second)
    loads[5].wait()
    loads[6].wait()
    mean, scale, shift = coefficients(packed, count, hr.shape[-1], gain_mid, shift_mid)
    activate_own(hr, ha, mean, scale, shift)
    wait_received(h_late)
    wait_received(h_early)
    activate_edges(hr, ha, 2, 6, mean, scale, shift)
    activate_past(hr, ha, mean, scale, shift)
    loads[7].wait()
    decoded = convolve(ha, w2, acc, 0, 4) + skip[...]
    out_ref[...] = decoded.reshape(out_ref.shape).astype(BF16)

    wait_sent(x_copies)
    wait_sent(h_late)
    wait_sent(h_early)
    for which in range(2):
        for stage in range(2):
            buffer = (stat_in_a, stat_in_b)[stage]
            pltpu.make_async_copy(
                buffer.at[which], buffer.at[which], stat_send.at[which, stage]
            ).wait()


def per_device(features, gain_in, shift_in, conv_in, gain_mid, shift_mid, conv_out, shortcut):
    c_in = features.shape[-1]
    c_out = shortcut.shape[-1]
    members = [len(offsets(axes)) for axes in STAGES]
    whole = pl.BlockSpec(memory_space=pl.ANY)
    return pl.pallas_call(
        kernel,
        out_shape=jax.ShapeDtypeStruct((FRAMES, ROWS, COLS, c_out), BF16),
        in_specs=[whole] * 8,
        out_specs=pl.BlockSpec(memory_space=pltpu.VMEM),
        scratch_shapes=[
            pltpu.VMEM((FRAMES + 2, ROWS + 2, COLS, c_in), BF16),
            pltpu.VMEM((FRAMES + 2, ROWS + 2, COLS, c_in), BF16),
            pltpu.VMEM((FRAMES + 2, ROWS + 2, COLS, c_out), BF16),
            pltpu.VMEM((FRAMES + 2, ROWS + 2, COLS, c_out), BF16),
            pltpu.VMEM(conv_in.shape, BF16),
            pltpu.VMEM(conv_out.shape, BF16),
            pltpu.VMEM(shortcut.shape, BF16),
            pltpu.VMEM((3, CELLS, c_out), F32),
            pltpu.VMEM((CELLS, c_out), F32),
            pltpu.VMEM((1, c_in), F32),
            pltpu.VMEM((1, c_in), F32),
            pltpu.VMEM((1, c_out), F32),
            pltpu.VMEM((1, c_out), F32),
            pltpu.VMEM((2, 2, 1, 128), F32),
            pltpu.VMEM((2, members[0], 1, 128), F32),
            pltpu.VMEM((2, members[1], 1, 128), F32),
            pltpu.SemaphoreType.DMA((8,)),
            pltpu.SemaphoreType.DMA((2, 2)),
            pltpu.SemaphoreType.DMA((2, 2)),
            pltpu.SemaphoreType.DMA((5,)),
            pltpu.SemaphoreType.DMA((5,)),
            pltpu.SemaphoreType.DMA((7,)),
            pltpu.SemaphoreType.DMA((7,)),
        ],
        compiler_params=pltpu.CompilerParams(
            collective_id=0, has_side_effects=True, vmem_limit_bytes=60 * 2**20
        ),
        name="residual_block",
    )(
        features, gain_in.reshape(1, -1), shift_in.reshape(1, -1), conv_in,
        gain_mid.reshape(1, -1), shift_mid.reshape(1, -1), conv_out, shortcut,
    )


def solution(mesh):
    return jax.shard_map(
        per_device,
        mesh=mesh,
        in_specs=(P("tm", "rows", None, None), P(), P(), P(), P(), P(), P(), P()),
        out_specs=P("tm", "rows", None, None),
        check_vma=False,
    )
```

time: 392 us -> 48.3 us (0.12)
  blocking collectives: 304 us -> 0 us
  Pallas kernels: 0 us -> 46.3 us
  local copies, waits for them, and re-layouts: 28.9 us -> 1.87 us
  starting transfers between devices: 17.1 us -> 0 us
  matrix products: 15.4 us -> 0 us
  other arithmetic: 13.7 us -> 0 us
  waiting for transfers between devices: 8.67 us -> 0 us
    psum x4 -> x0, blocking collectives: 304 us -> none  [the longest x2 159 us: statistics(): group_mean = lax.psum(partial_sum, ('tm', 'rows')) / cell_count]
    pallas_call x0 -> x1, Pallas kernels: none -> 46.3 us  [per_device(): pl.pallas_call(kernel, out_shape=jax.ShapeDtypeStruct((FRAMES, ROWS, COLS...]
    slice x9 -> x0, local copies, waits for them, and re-layouts: 18.6 us -> none  [the longest x5 10.3 us: conv_block(): extended[offset_time:offset_time + out_frames, offset_row:offset_row + ou...]
    ppermute x6 -> x0, starting transfers between devices: 17.1 us -> none  [the longest x2 8.82 us: extended_2(): lax.ppermute(tail, axis, [(i, (i + 1) % count) for i in range(ends)])]
    dot_general x19 -> x0, matrix products: 15.4 us -> none  [the longest x18 14.2 us: conv_block(): jnp.dot(stacked.reshape(-1, 3 * channels), matrix, preferred_element_type...]
    ppermute x6 -> x0, waiting for transfers between devices: 8.67 us -> none  [the longest x2 7.02 us: shifted(): return lax.ppermute(block, axis, route)]
    concatenate x22 -> x0, other arithmetic: 7.51 us -> none  [the longest x16 3.66 us: conv_block(): jnp.concatenate([extended[offset_time:offset_time + out_frames, offset_ro...]
    unnamed x46 -> x1, local copies, waits for them, and re-layouts: 9.29 us -> 1.87 us
  transfers between devices with their start and end apart: 6 -> 0, of which waited for: 3 -> 0; matrix products, arithmetic and copies ran while one was open for 2% -> 0% of each run, Pallas kernels for 0% -> 0%
where the time goes in v1:
time: 48.3 us; the launch traced here: 48.2 us
  Pallas kernels  46.3 us (96%)
  local copies, waits for them, and re-layouts  1.87 us (4%)
    pallas_call x1, Pallas kernels, per_device(): pl.pallas_call(kernel, out_shape=jax.ShapeDtypeStruct((FRAMES, ROWS, COLS...  46.3 us
    unnamed x1, local copies, waits for them, and re-layouts  1.87 us

profile of v1, /device:TPU:1, one launch (start us, length us, event | category | flops | bytes accessed | tf_op | source)
XLA Modules:
  0.0 48.2 jit_solution(6733759926906204634)
XLA Ops:
  0.0 46.3 %residual_block.1 = bf16[4,8,32,256]{3,2,1,0:T(8,128)(2,1)} custom-call(bf16[4,8,32,512]{3,2,1,0:T(8,128)(2,1)} %x_hbm.1, f32[1,512]{1,0:T(1,128)} %bitcast.4, f32[1,512]{1,0:T(1,128)} %bitcast.5, bf16[3,3,3,512,256]{4,3,2,1,0:T(8,128)(2,1)} %w1_hbm.1, f32[1,256]{1,0:T(1,128)} %bitcast.6, f32[1,256]{1,0:T(1,128)} %bitcast.7, ...), custom_call_target="tpu_custom_call" | custom-call | tf_op jit(solution)/shard_map/residual_block/pallas_call | solution.py:396
  46.3 1.9 %copy.10 = bf16[4,8,32,256]{3,2,1,0:T(8,128)(2,1)} copy(bf16[4,8,32,256]{3,2,1,0:T(8,128)(2,1)} %residual_block.1) | data formatting | bytes 1048576

commit v2 on v1

--- a/solution.py
+++ b/solution.py
@@ -17,7 +17,7 @@
 BF16 = jnp.bfloat16
 MESH = pl.DeviceIdType.MESH
 SIZES = {"y": 4, "x": 4, "core": 2, "z": 8}
-STAGES = (("z", "core"), ("y", "x"))
+STAGES = ((("z", "core"), ("y", "x")), (("core",), ("y", "x", "z")))
 HOPS = {2: (0, 1), 4: (0, 1, 2, 1), 8: (0, 1, 2, 3, 4, 3, 2, 1)}
 
 
@@ -99,38 +99,75 @@
 
 def activate_slab(raw, out, frame, row, mean, scale, shift):
     v = (raw[frame, row].astype(F32) - mean) * scale + shift
-    out[frame, row] = (v + v * jnp.tanh(v)).astype(BF16)
-
-
-def convolve(act, weights, acc, first_frame, frames):
+    out[frame, row % 2, row // 2] = (v + v * jnp.tanh(v)).astype(BF16)
+
+
+def transform_weights(weights, sums):
+    depth = weights.shape[3]
+    step = 64
+
+    def body(i, carry):
+        tap, part = i // (depth // step), i % (depth // step)
+        a, e = tap // 3, tap % 3
+        k = pl.ds(pl.multiple_of(part * step, step), step)
+        outer = weights[a, 0, e, k].astype(F32) + weights[a, 2, e, k].astype(F32)
+        middle = weights[a, 1, e, k].astype(F32)
+        sums[a, 0, e, k] = (outer + middle).astype(BF16)
+        sums[a, 1, e, k] = (outer - middle).astype(BF16)
+        return carry
+
+    lax.fori_loop(0, 9 * (depth // step), body, 0)
+
+
+def convolve(act, weights, sums, acc, hold, first_frame, frames):
     channels = act.shape[-1]
-    cells = frames * ROWS * COLS
+    width = weights.shape[-1]
+    half = ROWS // 2
+    cells = frames * half * COLS
 
     def one_column_tap(e, carry):
-        taps = [
-            act[first_frame + a : first_frame + a + frames, b : b + ROWS].reshape(cells, channels)
-            for a in range(3)
-            for b in range(3)
+        def rows(a, parity, k):
+            frame = first_frame + a
+            return act[frame : frame + frames, parity, k : k + half].reshape(cells, channels)
+
+        inputs = [
+            lambda a: rows(a, 0, 0) - rows(a, 0, 1),
+            lambda a: rows(a, 1, 0) + rows(a, 0, 1),
+            lambda a: rows(a, 0, 1) - rows(a, 1, 0),
+            lambda a: rows(a, 1, 0) - rows(a, 1, 1),
         ]
-        matrix = weights[:, :, e].reshape(9 * channels, weights.shape[-1])
-        acc[e, 0:cells] = jnp.dot(
-            jnp.concatenate(taps, axis=-1), matrix, preferred_element_type=F32
-        )
+        matrices = [weights[:, 0, e], sums[:, 0, e], sums[:, 1, e], weights[:, 2, e]]
+        for i in range(4):
+            taps = jnp.concatenate([inputs[i](a) for a in range(3)], axis=-1)
+            acc[e, i, 0:cells] = jnp.dot(
+                taps, matrices[i].reshape(3 * channels, width), preferred_element_type=F32
+            )
         return carry
 
     lax.fori_loop(0, 3, one_column_tap, 0)
-    left, middle, right = acc[0, 0:cells], acc[1, 0:cells], acc[2, 0:cells]
-    col = lax.broadcasted_iota(jnp.int32, left.shape, 0) % COLS
-    from_left = jnp.where(col == 0, 0.0, pltpu.roll(left, 1, 0))
-    from_right = jnp.where(col == COLS - 1, 0.0, pltpu.roll(right, cells - 1, 0))
-    return middle + from_left + from_right
+
+    def row_of(parity, e):
+        if parity == 0:
+            return acc[e, 0, 0:cells] + 0.5 * (acc[e, 1, 0:cells] + acc[e, 2, 0:cells])
+        return 0.5 * (acc[e, 1, 0:cells] - acc[e, 2, 0:cells]) - acc[e, 3, 0:cells]
+
+    for parity in range(2):
+        left, middle, right = (row_of(parity, e) for e in range(3))
+        col = lax.broadcasted_iota(jnp.int32, left.shape, 0) % COLS
+        from_left = jnp.where(col == 0, 0.0, pltpu.roll(left, 1, 0))
+        from_right = jnp.where(col == COLS - 1, 0.0, pltpu.roll(right, cells - 1, 0))
+        summed = middle + from_left + from_right
+        for f in range(frames):
+            for k in range(half):
+                start = (f * half + k) * COLS
+                hold(first_frame + f, 2 * k + parity, summed[start : start + COLS])
 
 
 def kernel(
     x_hbm, gain_in_hbm, shift_in_hbm, w1_hbm, gain_mid_hbm, shift_mid_hbm, w2_hbm, short_hbm,
     out_ref,
-    xr, xa, hr, ha, w1, w2, short, acc, skip, gain_in, shift_in, gain_mid, shift_mid,
-    stat_out, stat_in_a, stat_in_b,
+    xr, xa, hr, ha, w1, s1, w2, s2, short, acc, skip, gain_in, shift_in, gain_mid, shift_mid,
+    stat_out, stat_in_a, stat_in_b, stat_in_c, stat_in_d,
     load_sem, stat_send, stat_recv, x_send, x_recv, h_send, h_recv,
 ):
     tm = lax.axis_index("tm")
@@ -146,7 +183,10 @@
         return ((there["y"] * 4 + there["x"]) * 2 + there["core"], there["z"])
 
     barrier = pltpu.get_barrier_semaphore()
-    stage_partners = [[partner(axes, o) for o in offsets(axes)] for axes in STAGES]
+    stage_partners = [
+        [[partner(axes, o) for o in offsets(axes)] for axes in stages] for stages in STAGES
+    ]
+    stat_in = ((stat_in_a, stat_in_b), (stat_in_c, stat_in_d))
 
     loads = [
         pltpu.make_async_copy(src, dst, load_sem.at[i])
@@ -163,10 +203,9 @@
             ]
         )
     ]
-    for load in loads:
-        load.start()
-
-    for target in itertools.chain(*stage_partners):
+    loads[0].start()
+
+    for target in itertools.chain(*stage_partners[0]):
         pl.semaphore_signal(barrier, inc=1, device_id=target, device_id_type=MESH)
 
     def greet(ok, target):
@@ -235,28 +274,25 @@
             pl.when(gets)(copy.wait_recv)
 
     def stat_copies(which, stage):
-        buffer = (stat_in_a, stat_in_b)[stage]
         return [
             pltpu.make_async_remote_copy(
-                src_ref=stat_out.at[which, stage], dst_ref=buffer.at[which, i],
+                src_ref=stat_out.at[which, stage], dst_ref=stat_in[which][stage].at[i],
                 send_sem=stat_send.at[which, stage], recv_sem=stat_recv.at[which, stage],
                 device_id=target, device_id_type=MESH,
             )
-            for i, target in enumerate(stage_partners[stage])
+            for i, target in enumerate(stage_partners[which][stage])
         ]
 
     def exchange(which, packed, count, meanwhile):
         for stage in range(2):
-            buffer = (stat_in_a, stat_in_b)[stage]
+            buffer = stat_in[which][stage]
             stat_out[which, stage] = packed
             for copy in stat_copies(which, stage):
                 copy.start()
             meanwhile(stage)
-            pltpu.make_async_copy(
-                buffer.at[which], buffer.at[which], stat_recv.at[which, stage]
-            ).wait()
-            packed = combined(packed, buffer[which], count)
-            count = count * (buffer.shape[1] + 1)
+            pltpu.make_async_copy(buffer, buffer, stat_recv.at[which, stage]).wait()
+            packed = combined(packed, buffer[...], count)
+            count = count * (buffer.shape[0] + 1)
         return packed, count
 
     def coefficients(packed, count, channels, gain, shift):
@@ -284,7 +320,7 @@
 
             @pl.when(jnp.logical_not(ok))
             def _():
-                out[lo:hi, row] = jnp.zeros((hi - lo, COLS, out.shape[-1]), BF16)
+                out[lo:hi, row % 2, row // 2] = jnp.zeros((hi - lo, COLS, out.shape[-1]), BF16)
 
     def activate_past(raw, out, mean, scale, shift):
         @pl.when(has_prev)
@@ -299,8 +335,8 @@
         @pl.when(jnp.logical_not(has_prev))
         def _():
             def body(r, carry):
-                out[0, r] = out[2, r]
-                out[1, r] = out[2, r]
+                out[0, r % 2, r // 2] = out[2, r % 2, r // 2]
+                out[1, r % 2, r // 2] = out[2, r % 2, r // 2]
                 return carry
 
             lax.fori_loop(0, ROWS + 2, body, 0)
@@ -324,10 +360,12 @@
     )
 
     loads[0].wait()
+    for load in loads[1:]:
+        load.start()
     packed = local_statistics(xr)
     pl.semaphore_wait(
         barrier,
-        sum(len(p) for p in stage_partners)
+        sum(len(p) for p in stage_partners[0])
         + has_next.astype(jnp.int32)
         + (has_next & has_above).astype(jnp.int32)
         + (has_next & has_below).astype(jnp.int32),
@@ -339,8 +377,12 @@
             skip[...] = jnp.dot(
                 xr[2:6, 1:9].reshape(CELLS, xr.shape[-1]), short[...], preferred_element_type=F32
             )
+            loads[7].wait()
+            transform_weights(w2, s2)
         if stage == 1:
             start(x_copies)
+            loads[4].wait()
+            transform_weights(w1, s1)
 
     packed, count = exchange(0, packed, CELLS * (xr.shape[-1] // GROUPS), during_first)
     loads[1].wait()
@@ -349,14 +391,15 @@
     activate_own(xr, xa, mean, scale, shift)
     wait_received(x_copies[:2])
     activate_edges(xr, xa, 2, 6, mean, scale, shift)
-    loads[4].wait()
-    hidden = convolve(xa, w1, acc, 2, 2)
-    hr[4:6, 1:9] = hidden.reshape(2, ROWS, COLS, hidden.shape[-1]).astype(BF16)
+
+    def hold_hidden(frame, row, values):
+        hr[2 + frame, 1 + row] = values.astype(BF16)
+
+    convolve(xa, w1, s1, acc, hold_hidden, 2, 2)
     start(h_late)
     wait_received(x_copies[2:])
     activate_past(xr, xa, mean, scale, shift)
-    hidden = convolve(xa, w1, acc, 0, 2)
-    hr[2:4, 1:9] = hidden.reshape(2, ROWS, COLS, hidden.shape[-1]).astype(BF16)
+    convolve(xa, w1, s1, acc, hold_hidden, 0, 2)
 
     packed = local_statistics(hr)
 
@@ -373,48 +416,51 @@
     wait_received(h_early)
     activate_edges(hr, ha, 2, 6, mean, scale, shift)
     activate_past(hr, ha, mean, scale, shift)
-    loads[7].wait()
-    decoded = convolve(ha, w2, acc, 0, 4) + skip[...]
-    out_ref[...] = decoded.reshape(out_ref.shape).astype(BF16)
+
+    def hold_decoded(frame, row, values):
+        cell = (frame * ROWS + row) * COLS
+        out_ref[frame, row] = (values + skip[cell : cell + COLS]).astype(BF16)
+
+    convolve(ha, w2, s2, acc, hold_decoded, 0, 4)
 
     wait_sent(x_copies)
     wait_sent(h_late)
     wait_sent(h_early)
     for which in range(2):
         for stage in range(2):
-            buffer = (stat_in_a, stat_in_b)[stage]
-            pltpu.make_async_copy(
-                buffer.at[which], buffer.at[which], stat_send.at[which, stage]
-            ).wait()
+            buffer = stat_in[which][stage]
+            pltpu.make_async_copy(buffer, buffer, stat_send.at[which, stage]).wait()
 
 
 def per_device(features, gain_in, shift_in, conv_in, gain_mid, shift_mid, conv_out, shortcut):
     c_in = features.shape[-1]
     c_out = shortcut.shape[-1]
-    members = [len(offsets(axes)) for axes in STAGES]
+    members = [len(offsets(axes)) for stages in STAGES for axes in stages]
+    half = (ROWS + 2) // 2
     whole = pl.BlockSpec(memory_space=pl.ANY)
     return pl.pallas_call(
         kernel,
-        out_shape=jax.ShapeDtypeStruct((FRAMES, ROWS, COLS, c_out), BF16),
+        out_shape=pltpu.VMEM((FRAMES, ROWS, COLS, c_out), BF16),
         in_specs=[whole] * 8,
         out_specs=pl.BlockSpec(memory_space=pltpu.VMEM),
         scratch_shapes=[
             pltpu.VMEM((FRAMES + 2, ROWS + 2, COLS, c_in), BF16),
-            pltpu.VMEM((FRAMES + 2, ROWS + 2, COLS, c_in), BF16),
+            pltpu.VMEM((FRAMES + 2, 2, half, COLS, c_in), BF16),
             pltpu.VMEM((FRAMES + 2, ROWS + 2, COLS, c_out), BF16),
-            pltpu.VMEM((FRAMES + 2, ROWS + 2, COLS, c_out), BF16),
+            pltpu.VMEM((FRAMES + 2, 2, half, COLS, c_out), BF16),
             pltpu.VMEM(conv_in.shape, BF16),
+            pltpu.VMEM((3, 2, 3, c_in, c_out), BF16),
             pltpu.VMEM(conv_out.shape, BF16),
+            pltpu.VMEM((3, 2, 3, c_out, c_out), BF16),
             pltpu.VMEM(shortcut.shape, BF16),
-            pltpu.VMEM((3, CELLS, c_out), F32),
+            pltpu.VMEM((3, 4, CELLS // 2, c_out), F32),
             pltpu.VMEM((CELLS, c_out), F32),
             pltpu.VMEM((1, c_in), F32),
             pltpu.VMEM((1, c_in), F32),
             pltpu.VMEM((1, c_out), F32),
             pltpu.VMEM((1, c_out), F32),
             pltpu.VMEM((2, 2, 1, 128), F32),
-            pltpu.VMEM((2, members[0], 1, 128), F32),
-            pltpu.VMEM((2, members[1], 1, 128), F32),
+            *[pltpu.VMEM((count, 1, 128), F32) for count in members],
             pltpu.SemaphoreType.DMA((8,)),
             pltpu.SemaphoreType.DMA((2, 2)),
             pltpu.SemaphoreType.DMA((2, 2)),

time: 48.3 us -> 43 us (0.89)
  Pallas kernels: 46.3 us -> 42.1 us
  local copies, waits for them, and re-layouts: 1.87 us -> 0.8 us
    pallas_call x1, Pallas kernels: 46.3 us -> 42.1 us  [per_device(): pl.pallas_call(kernel, out_shape=pltpu.VMEM((FRAMES, ROWS, COLS, c_out),...]
    unnamed x1, local copies, waits for them, and re-layouts: 1.87 us -> 0.8 us
where the time goes in v2:
time: 43 us; the launch traced here: 42.9 us
  Pallas kernels  42.1 us (98%)
  local copies, waits for them, and re-layouts  0.8 us (2%)
    pallas_call x1, Pallas kernels, per_device(): pl.pallas_call(kernel, out_shape=pltpu.VMEM((FRAMES, ROWS, COLS, c_out),...  42.1 us

profile of v2, /device:TPU:1, one launch (start us, length us, event | category | flops | bytes accessed | tf_op | source)
XLA Modules:
  0.0 42.9 jit_solution(10716151003510873285)
XLA Ops:
  0.0 42.1 %residual_block.1 = bf16[4,8,32,256]{3,2,1,0:T(8,128)(2,1)S(1)} custom-call(bf16[4,8,32,512]{3,2,1,0:T(8,128)(2,1)} %x_hbm.1, f32[1,512]{1,0:T(1,128)} %bitcast.4, f32[1,512]{1,0:T(1,128)} %bitcast.5, bf16[3,3,3,512,256]{4,3,2,1,0:T(8,128)(2,1)} %w1_hbm.1, f32[1,256]{1,0:T(1,128)} %bitcast.6, f32[1,256]{1,0:T(1,128)} %bitcast.7, ...), custom_call_target="tpu_custom_call" | custom-call | tf_op jit(solution)/shard_map/residual_block/pallas_call | solution.py:441
  42.1 0.8 %copy.10 = bf16[4,8,32,256]{3,2,1,0:T(8,128)(2,1)} copy(bf16[4,8,32,256]{3,2,1,0:T(8,128)(2,1)S(1)} %residual_block.1) | data formatting | bytes 1048576

commit v3 on v2

--- a/solution.py
+++ b/solution.py
@@ -17,6 +17,7 @@
 BF16 = jnp.bfloat16
 MESH = pl.DeviceIdType.MESH
 SIZES = {"y": 4, "x": 4, "core": 2, "z": 8}
+UNROLL = 8
 STAGES = ((("z", "core"), ("y", "x")), (("core",), ("y", "x", "z")))
 HOPS = {2: (0, 1), 4: (0, 1, 2, 1), 8: (0, 1, 2, 3, 4, 3, 2, 1)}
 
@@ -46,43 +47,71 @@
     return jnp.concatenate([values[i : i + 1, :] for i in range(values.shape[0])], axis=1)
 
 
-def local_statistics(ext):
+def group_pivot(ext, frame):
     channels = ext.shape[-1]
     width = channels // GROUPS
+    cell = to_rows(ext[frame, 1].astype(F32)[0:1])
+    lane = lax.broadcasted_iota(jnp.int32, cell.shape, 1)
+    return group_sum(jnp.where(lane % width == 0, cell, 0.0), width)
+
+
+def add_up(ext, first, frames, pivot, sums):
+    channels = ext.shape[-1]
+    slabs = 4
+
+    def body(i, carry):
+        total, spread = carry
+        for j in range(slabs):
+            n = i * slabs + j
+            moved = ext[first + n // ROWS, 1 + n % ROWS].astype(F32) - pivot
+            parts = moved.reshape(COLS // 8, 8, channels)
+            total = total + parts.sum(0)
+            spread = spread + jnp.square(parts).sum(0)
+        return total, spread
+
+    return lax.fori_loop(0, frames * ROWS // slabs, body, sums)
+
+
+def no_sums(channels):
+    return jnp.zeros((8, channels), F32), jnp.zeros((8, channels), F32)
+
+
+def packed_statistics(pivot, sums):
+    total, spread = sums
+    channels = total.shape[-1]
+    width = channels // GROUPS
     rows = channels // 128
-
-    def slab(i):
-        return ext[2 + i // ROWS, 1 + i % ROWS].astype(F32)
-
-    def add_up(i, total):
-        return total + slab(i).reshape(COLS // 8, 8, channels).sum(0)
-
-    zero = jnp.zeros((8, channels), F32)
-    total = lax.fori_loop(0, FRAMES * ROWS, add_up, zero, unroll=4).sum(0, keepdims=True)
-    mean = group_sum(to_rows(total), width) * (1.0 / (CELLS * width))
-    wide_mean = to_lanes(mean)
-
-    def add_square(i, total):
-        return total + jnp.square(slab(i) - wide_mean).reshape(COLS // 8, 8, channels).sum(0)
-
-    spread = lax.fori_loop(0, FRAMES * ROWS, add_square, zero, unroll=4).sum(0, keepdims=True)
-    spread = group_sum(to_rows(spread), width)
+    both = jnp.concatenate(
+        [to_rows(total.sum(0, keepdims=True)), to_rows(spread.sum(0, keepdims=True))], axis=0
+    )
+    both = group_sum(both, width)
+    offset = both[:rows] * (1.0 / (CELLS * width))
+    mean = pivot + offset
+    spread = both[rows:] - both[:rows] * offset
     lane = lax.broadcasted_iota(jnp.int32, (1, 128), 1)
     packed = jnp.zeros((1, 128), F32)
     for r in range(rows):
-        both = jnp.where(lane % 4 < 2, mean[r : r + 1], spread[r : r + 1])
-        packed = packed + jnp.where((lane % width) // 4 == r, both, 0.0)
+        pair = jnp.where(lane % 4 < 2, mean[r : r + 1], spread[r : r + 1])
+        packed = packed + jnp.where((lane % width) // 4 == r, pair, 0.0)
     return packed
 
 
 def combined(own, others, count):
-    members = others.shape[0] + 1
+    held = others.shape[0] * others.shape[1]
+    full = held % 2 == 0
+    members = held if full else held + 1
     lane = lax.broadcasted_iota(jnp.int32, (1, 128), 1)
-    total = own + jnp.sum(others, axis=0)
+
+    def over_all(values):
+        return jnp.sum(jnp.sum(values, axis=0), axis=0, keepdims=True)
+
+    total = over_all(others) if full else own + over_all(others)
     mean = total * (1.0 / members)
-    deviation = jnp.square(own - mean) + jnp.sum(jnp.square(others - mean[None]), axis=0)
+    deviation = over_all(jnp.square(others - mean[None]))
+    if not full:
+        deviation = deviation + jnp.square(own - mean)
     moved = pltpu.roll(deviation, 2, 1)
-    return jnp.where(lane % 4 < 2, mean, total + moved * float(count))
+    return jnp.where(lane % 4 < 2, mean, total + moved * float(count)), members
 
 
 def unpacked(packed, channels):
@@ -110,8 +139,8 @@
         tap, part = i // (depth // step), i % (depth // step)
         a, e = tap // 3, tap % 3
         k = pl.ds(pl.multiple_of(part * step, step), step)
-        outer = weights[a, 0, e, k].astype(F32) + weights[a, 2, e, k].astype(F32)
-        middle = weights[a, 1, e, k].astype(F32)
+        outer = 0.5 * (weights[a, 0, e, k].astype(F32) + weights[a, 2, e, k].astype(F32))
+        middle = 0.5 * weights[a, 1, e, k].astype(F32)
         sums[a, 0, e, k] = (outer + middle).astype(BF16)
         sums[a, 1, e, k] = (outer - middle).astype(BF16)
         return carry
@@ -124,50 +153,56 @@
     width = weights.shape[-1]
     half = ROWS // 2
     cells = frames * half * COLS
-
-    def one_column_tap(e, carry):
-        def rows(a, parity, k):
-            frame = first_frame + a
-            return act[frame : frame + frames, parity, k : k + half].reshape(cells, channels)
-
-        inputs = [
-            lambda a: rows(a, 0, 0) - rows(a, 0, 1),
-            lambda a: rows(a, 1, 0) + rows(a, 0, 1),
-            lambda a: rows(a, 0, 1) - rows(a, 1, 0),
-            lambda a: rows(a, 1, 0) - rows(a, 1, 1),
-        ]
+    col = lax.broadcasted_iota(jnp.int32, (COLS, width), 0)
+
+    def rows(a, parity, k):
+        frame = first_frame + a
+        return act[frame : frame + frames, parity, k : k + half].reshape(cells, channels)
+
+    inputs = [
+        lambda a: rows(a, 0, 0) - rows(a, 0, 1),
+        lambda a: rows(a, 1, 0) + rows(a, 0, 1),
+        lambda a: rows(a, 0, 1) - rows(a, 1, 0),
+        lambda a: rows(a, 1, 0) - rows(a, 1, 1),
+    ]
+
+    def one_column_tap(e):
         matrices = [weights[:, 0, e], sums[:, 0, e], sums[:, 1, e], weights[:, 2, e]]
         for i in range(4):
             taps = jnp.concatenate([inputs[i](a) for a in range(3)], axis=-1)
             acc[e, i, 0:cells] = jnp.dot(
                 taps, matrices[i].reshape(3 * channels, width), preferred_element_type=F32
             )
-        return carry
-
-    lax.fori_loop(0, 3, one_column_tap, 0)
-
-    def row_of(parity, e):
-        if parity == 0:
-            return acc[e, 0, 0:cells] + 0.5 * (acc[e, 1, 0:cells] + acc[e, 2, 0:cells])
-        return 0.5 * (acc[e, 1, 0:cells] - acc[e, 2, 0:cells]) - acc[e, 3, 0:cells]
-
-    for parity in range(2):
-        left, middle, right = (row_of(parity, e) for e in range(3))
-        col = lax.broadcasted_iota(jnp.int32, left.shape, 0) % COLS
-        from_left = jnp.where(col == 0, 0.0, pltpu.roll(left, 1, 0))
-        from_right = jnp.where(col == COLS - 1, 0.0, pltpu.roll(right, cells - 1, 0))
-        summed = middle + from_left + from_right
-        for f in range(frames):
-            for k in range(half):
-                start = (f * half + k) * COLS
-                hold(first_frame + f, 2 * k + parity, summed[start : start + COLS])
+
+    def pair_of_rows(e, slab):
+        m = [acc[e, i, slab] for i in range(4)]
+        return m[0] + (m[1] + m[2]), (m[1] - m[2]) - m[3]
+
+    places = [
+        (f, k, slice((f * half + k) * COLS, (f * half + k + 1) * COLS))
+        for f in range(frames)
+        for k in range(half)
+    ]
+    one_column_tap(0)
+    one_column_tap(1)
+    for _, _, slab in places:
+        left, middle = pair_of_rows(0, slab), pair_of_rows(1, slab)
+        for parity in range(2):
+            from_left = jnp.where(col == 0, 0.0, pltpu.roll(left[parity], 1, 0))
+            acc[0, parity, slab] = middle[parity] + from_left
+    one_column_tap(2)
+    for f, k, slab in places:
+        right = pair_of_rows(2, slab)
+        for parity in range(2):
+            from_right = jnp.where(col == COLS - 1, 0.0, pltpu.roll(right[parity], COLS - 1, 0))
+            hold(first_frame + f, 2 * k + parity, acc[0, parity, slab] + from_right)
 
 
 def kernel(
     x_hbm, gain_in_hbm, shift_in_hbm, w1_hbm, gain_mid_hbm, shift_mid_hbm, w2_hbm, short_hbm,
     out_ref,
     xr, xa, hr, ha, w1, s1, w2, s2, short, acc, skip, gain_in, shift_in, gain_mid, shift_mid,
-    stat_out, stat_in_a, stat_in_b, stat_in_c, stat_in_d,
+    stat_out, stat_size, stat_in_a, stat_in_b, stat_in_c, stat_in_d,
     load_sem, stat_send, stat_recv, x_send, x_recv, h_send, h_recv,
 ):
     tm = lax.axis_index("tm")
@@ -192,7 +227,7 @@
         pltpu.make_async_copy(src, dst, load_sem.at[i])
         for i, (src, dst) in enumerate(
             [
-                (x_hbm, xr.at[2:6, 1:9]),
+                (x_hbm.at[0], xr.at[2, 1:9]),
                 (gain_in_hbm, gain_in),
                 (shift_in_hbm, shift_in),
                 (short_hbm, short),
@@ -200,10 +235,15 @@
                 (gain_mid_hbm, gain_mid),
                 (shift_mid_hbm, shift_mid),
                 (w2_hbm, w2),
+                (x_hbm.at[1], xr.at[3, 1:9]),
+                (x_hbm.at[2], xr.at[4, 1:9]),
+                (x_hbm.at[3], xr.at[5, 1:9]),
             ]
         )
     ]
-    loads[0].start()
+    frame_loads = [loads[0], *loads[8:]]
+    for load in frame_loads:
+        load.start()
 
     for target in itertools.chain(*stage_partners[0]):
         pl.semaphore_signal(barrier, inc=1, device_id=target, device_id_type=MESH)
@@ -273,15 +313,23 @@
         for _, gets, copy in copies:
             pl.when(gets)(copy.wait_recv)
 
+    def slot_of(buffer, i):
+        depth = buffer.shape[1]
+        return buffer.at[i // depth, i % depth : i % depth + 1]
+
     def stat_copies(which, stage):
         return [
             pltpu.make_async_remote_copy(
-                src_ref=stat_out.at[which, stage], dst_ref=stat_in[which][stage].at[i],
+                src_ref=stat_out.at[which, stage], dst_ref=slot_of(stat_in[which][stage], i),
                 send_sem=stat_send.at[which, stage], recv_sem=stat_recv.at[which, stage],
                 device_id=target, device_id_type=MESH,
             )
             for i, target in enumerate(stage_partners[which][stage])
         ]
+
+    def wait_for(which, stage, sems):
+        size = stat_size.at[0 : len(stage_partners[which][stage])]
+        pltpu.make_async_copy(size, size, sems.at[which, stage]).wait()
 
     def exchange(which, packed, count, meanwhile):
         for stage in range(2):
@@ -290,9 +338,11 @@
             for copy in stat_copies(which, stage):
                 copy.start()
             meanwhile(stage)
-            pltpu.make_async_copy(buffer, buffer, stat_recv.at[which, stage]).wait()
-            packed = combined(packed, buffer[...], count)
-            count = count * (buffer.shape[0] + 1)
+            if buffer.shape[1] > 1:
+                slot_of(buffer, len(stage_partners[which][stage]))[...] = packed
+            wait_for(which, stage, stat_recv)
+            packed, members = combined(packed, buffer[...], count)
+            count = count * members
         return packed, count
 
     def coefficients(packed, count, channels, gain, shift):
@@ -305,18 +355,15 @@
             activate_slab(raw, out, 2 + i // ROWS, 1 + i % ROWS, mean, scale, shift)
             return carry
 
-        lax.fori_loop(0, FRAMES * ROWS, body, 0, unroll=2)
+        lax.fori_loop(0, FRAMES * ROWS, body, 0, unroll=UNROLL)
 
     def activate_edges(raw, out, lo, hi, mean, scale, shift):
         for row, ok in ((0, has_above), (9, has_below)):
 
             @pl.when(ok)
             def _():
-                def body(f, carry):
+                for f in range(lo, hi):
                     activate_slab(raw, out, f, row, mean, scale, shift)
-                    return carry
-
-                lax.fori_loop(lo, hi, body, 0)
 
             @pl.when(jnp.logical_not(ok))
             def _():
@@ -329,7 +376,7 @@
                 activate_slab(raw, out, i // ROWS, 1 + i % ROWS, mean, scale, shift)
                 return carry
 
-            lax.fori_loop(0, 2 * ROWS, body, 0, unroll=2)
+            lax.fori_loop(0, 2 * ROWS, body, 0, unroll=UNROLL)
             activate_edges(raw, out, 0, 2, mean, scale, shift)
 
         @pl.when(jnp.logical_not(has_prev))
@@ -359,10 +406,16 @@
         own_hidden, hr, h_send, h_recv, [("down", "early", 5), ("up", "early", 6)]
     )
 
-    loads[0].wait()
-    for load in loads[1:]:
+    frame_loads[0].wait()
+    pivot = group_pivot(xr, 2)
+    sums = no_sums(xr.shape[-1])
+    for f in range(FRAMES):
+        if f > 0:
+            frame_loads[f].wait()
+        sums = add_up(xr, 2 + f, 1, to_lanes(pivot), sums)
+    for load in loads[1:8]:
         load.start()
-    packed = local_statistics(xr)
+    packed = packed_statistics(pivot, sums)
     pl.semaphore_wait(
         barrier,
         sum(len(p) for p in stage_partners[0])
@@ -397,11 +450,14 @@
 
     convolve(xa, w1, s1, acc, hold_hidden, 2, 2)
     start(h_late)
+    pivot = group_pivot(hr, 4)
+    sums = add_up(hr, 4, 2, to_lanes(pivot), no_sums(hr.shape[-1]))
     wait_received(x_copies[2:])
     activate_past(xr, xa, mean, scale, shift)
     convolve(xa, w1, s1, acc, hold_hidden, 0, 2)
 
-    packed = local_statistics(hr)
+    sums = add_up(hr, 2, 2, to_lanes(pivot), sums)
+    packed = packed_statistics(pivot, sums)
 
     def during_second(stage):
         if stage == 0:
@@ -428,14 +484,12 @@
     wait_sent(h_early)
     for which in range(2):
         for stage in range(2):
-            buffer = stat_in[which][stage]
-            pltpu.make_async_copy(buffer, buffer, stat_send.at[which, stage]).wait()
+            wait_for(which, stage, stat_send)
 
 
 def per_device(features, gain_in, shift_in, conv_in, gain_mid, shift_mid, conv_out, shortcut):
     c_in = features.shape[-1]
     c_out = shortcut.shape[-1]
-    members = [len(offsets(axes)) for stages in STAGES for axes in stages]
     half = (ROWS + 2) // 2
     whole = pl.BlockSpec(memory_space=pl.ANY)
     return pl.pallas_call(
@@ -460,8 +514,9 @@
             pltpu.VMEM((1, c_out), F32),
             pltpu.VMEM((1, c_out), F32),
             pltpu.VMEM((2, 2, 1, 128), F32),
-            *[pltpu.VMEM((count, 1, 128), F32) for count in members],
-            pltpu.SemaphoreType.DMA((8,)),
+            pltpu.VMEM((127, 1, 128), F32),
+            *[pltpu.VMEM((*slots, 128), F32) for slots in ((15, 1), (15, 1), (1, 1), (16, 8))],
+            pltpu.SemaphoreType.DMA((11,)),
             pltpu.SemaphoreType.DMA((2, 2)),
             pltpu.SemaphoreType.DMA((2, 2)),
             pltpu.SemaphoreType.DMA((5,)),

time: 43 us -> 40.8 us (0.949)
  Pallas kernels: 42.1 us -> 39.9 us
    pallas_call x1, Pallas kernels: 42.1 us -> 39.9 us  [per_device(): pl.pallas_call(kernel, out_shape=pltpu.VMEM((FRAMES, ROWS, COLS, c_out),...]
where the time goes in v3:
time: 40.8 us; the launch traced here: 40.7 us
  Pallas kernels  39.9 us (98%)
  local copies, waits for them, and re-layouts  0.8 us (2%)
    pallas_call x1, Pallas kernels, per_device(): pl.pallas_call(kernel, out_shape=pltpu.VMEM((FRAMES, ROWS, COLS, c_out),...  39.9 us

profile of v3, /device:TPU:1, one launch (start us, length us, event | category | flops | bytes accessed | tf_op | source)
XLA Modules:
  0.0 40.7 jit_solution(9924080884996752031)
XLA Ops:
  0.0 39.9 %residual_block.1 = bf16[4,8,32,256]{3,2,1,0:T(8,128)(2,1)S(1)} custom-call(bf16[4,8,32,512]{3,2,1,0:T(8,128)(2,1)} %x_hbm.1, f32[1,512]{1,0:T(1,128)} %bitcast.4, f32[1,512]{1,0:T(1,128)} %bitcast.5, bf16[3,3,3,512,256]{4,3,2,1,0:T(8,128)(2,1)} %w1_hbm.1, f32[1,256]{1,0:T(1,128)} %bitcast.6, f32[1,256]{1,0:T(1,128)} %bitcast.7, ...), custom_call_target="tpu_custom_call" | custom-call | tf_op jit(solution)/shard_map/residual_block/pallas_call | solution.py:495
  39.9 0.8 %copy.10 = bf16[4,8,32,256]{3,2,1,0:T(8,128)(2,1)} copy(bf16[4,8,32,256]{3,2,1,0:T(8,128)(2,1)S(1)} %residual_block.1) | data formatting | bytes 1048576

commit v4 on v3

--- a/solution.py
+++ b/solution.py
@@ -449,7 +449,6 @@
         hr[2 + frame, 1 + row] = values.astype(BF16)
 
     convolve(xa, w1, s1, acc, hold_hidden, 2, 2)
-    start(h_late)
     pivot = group_pivot(hr, 4)
     sums = add_up(hr, 4, 2, to_lanes(pivot), no_sums(hr.shape[-1]))
     wait_received(x_copies[2:])
@@ -460,7 +459,8 @@
     packed = packed_statistics(pivot, sums)
 
     def during_second(stage):
-        if stage == 0:
+        if stage == 1:
+            start(h_late)
             start(h_early)
 
     packed, count = exchange(1, packed, CELLS * (hr.shape[-1] // GROUPS), during_second)

time: 40.8 us -> 40.5 us (level)
  no operation moved by 1% of the time
where the time goes in v4:
time: 40.5 us
  Pallas kernels  39.7 us (98%)
  local copies, waits for them, and re-layouts  0.8 us (2%)
    pallas_call x1, Pallas kernels, per_device(): pl.pallas_call(kernel, out_shape=pltpu.VMEM((FRAMES, ROWS, COLS, c_out),...  39.7 us

profile of v4, /device:TPU:1, one launch (start us, length us, event | category | flops | bytes accessed | tf_op | source)
XLA Modules:
  0.0 40.5 jit_solution(14949726003688644450)
XLA Ops:
  0.0 39.7 %residual_block.1 = bf16[4,8,32,256]{3,2,1,0:T(8,128)(2,1)S(1)} custom-call(bf16[4,8,32,512]{3,2,1,0:T(8,128)(2,1)} %x_hbm.1, f32[1,512]{1,0:T(1,128)} %bitcast.4, f32[1,512]{1,0:T(1,128)} %bitcast.5, bf16[3,3,3,512,256]{4,3,2,1,0:T(8,128)(2,1)} %w1_hbm.1, f32[1,256]{1,0:T(1,128)} %bitcast.6, f32[1,256]{1,0:T(1,128)} %bitcast.7, ...), custom_call_target="tpu_custom_call" | custom-call | tf_op jit(solution)/shard_map/residual_block/pallas_call | solution.py:495
  39.7 0.8 %copy.10 = bf16[4,8,32,256]{3,2,1,0:T(8,128)(2,1)} copy(bf16[4,8,32,256]{3,2,1,0:T(8,128)(2,1)S(1)} %residual_block.1) | data formatting | bytes 1048576
